TPU v7x, 32 devices: a whole 2x2x4 slice. The times are simulated.
32 devices in a mesh: groups: 2 (over y), expert: 4 (over z), dp: 2 (over x), tensor: 2 (over core).
Axes of the slice: x: 2, y: 2, z: 4, core: 2. Of those that a mesh axis runs over, the one named last changes fastest.
Arguments:
- hidden: bfloat16 [32, 2, 4, 80, 768], P(('groups', 'expert'), 'dp', None, None, 'tensor'), parts along dimension 0, may hold values from -6 to 6
- frozen_a: bfloat16 [16, 768, 64], P('expert', 'tensor'), may hold values from -0.21875 to 0.21875
- trained_b: bfloat16 [16, 64, 4096], P('expert', None, 'tensor'), may hold values from -0.75 to 0.75
- routes: int32 [2048, 8], P(('groups', 'expert', 'dp')), parts along dimension 0, may hold values from 0 to 15, all different within a row; in each aligned block of 128 rows (0 to 127, 128 to 255, ...) at most 80 rows name the same one
- gate_weights: float32 [2048, 8], P(('groups', 'expert', 'dp')), parts along dimension 0, may hold values from 0.05 to 0.5
- cotangent: bfloat16 [2048, 4096], P(('groups', 'expert', 'dp'), 'tensor'), parts along dimension 0, may hold values from -6 to 6
Outputs:
- adapter_out: bfloat16 [2048, 4096], P(('groups', 'expert', 'dp'), 'tensor'), parts along dimension 0
- adapter_grad: float32 [32, 64, 4096], P(('groups', 'expert'), 'dp', 'tensor'), parts along dimension 0
- hidden_grad: bfloat16 [32, 2, 4, 80, 768], P(('groups', 'expert'), 'dp', None, None, 'tensor'), parts along dimension 0
There are 2 independent parts, one for each index of `groups`. A program takes and returns all parts, laid end to end along the dimension named above; an argument that names none is the same for every part. Nothing has to cross between parts.
Inputs may be any that keep to these rules, and one draw needn't show every extreme that they name: `routes`: in each aligned block of 128 rows (the rows of one device), no expert is named by more than 80 rows, a bound that some block reaches. Each row names 8 different experts.
All inputs are finite; a program needn't handle non-finite values.
Results may differ from a plain program's by a relative error of at most 0.0057.
Values may be sent and summed in bfloat16 or wider, within the bound.
A program may use at most 128 MiB of HBM per device.

v0:
```python
import jax
import jax.numpy as jnp
from jax import lax
from jax.sharding import PartitionSpec as P


def route_slots(routes, experts_all):
    experts = jnp.arange(experts_all, dtype=jnp.int32)
    hit_count = jnp.sum((routes[:, :, None] == experts).astype(jnp.int32), axis=1)
    before = jnp.cumsum(hit_count, axis=0) - hit_count
    return jnp.take_along_axis(before, routes, axis=1)


def build_at_experts(routes, gate_weights, cotangent, local_experts, capacity, experts_all):
    blocks = lax.axis_size("expert")
    tok_rows = routes.shape[0]
    half_width = cotangent.shape[1]
    all_cot = lax.all_gather(cotangent, "expert", axis=0, tiled=True)
    all_routes = lax.all_gather(routes, "expert", axis=0, tiled=True)
    all_gates = lax.all_gather(gate_weights, "expert", axis=0, tiled=True)
    grouped = all_routes.reshape(blocks, tok_rows, routes.shape[1])
    places = jax.vmap(route_slots, in_axes=(0, None))(grouped, experts_all)
    local_index = grouped - lax.axis_index("expert") * local_experts
    inside = (local_index >= 0) & (local_index < local_experts)
    block_id = lax.broadcasted_iota(jnp.int32, grouped.shape, 0)
    token_id = block_id * tok_rows + lax.broadcasted_iota(jnp.int32, grouped.shape, 1)
    slot_total = blocks * local_experts * capacity
    target = jnp.where(
        inside, (block_id * local_experts + local_index) * capacity + places, slot_total
    )
    target = target.reshape(-1)
    source = (
        jnp.zeros((slot_total + 1,), jnp.int32).at[target].set(token_id.reshape(-1))[:slot_total]
    )
    weight = (
        jnp.zeros((slot_total + 1,), jnp.float32).at[target].set(all_gates.reshape(-1))[:slot_total]
    )
    slot_rows = (weight[:, None] * all_cot[source].astype(jnp.float32)).astype(jnp.bfloat16)
    return slot_rows.reshape(blocks, local_experts, capacity, half_width)


def local(hidden, frozen_a, trained_b, routes, gate_weights, cotangent):
    local_experts = frozen_a.shape[0]
    experts_all = local_experts * lax.axis_size("expert")
    capacity = hidden.shape[3]
    half_width = trained_b.shape[2]
    tok_rows = routes.shape[0]
    top_count = routes.shape[1]
    slot_place = route_slots(routes, experts_all)
    flat_index = routes * capacity + slot_place
    hidden_rows = hidden[:, 0]
    partial_low = jnp.einsum(
        "xscf,xfr->sxcr", hidden_rows, frozen_a, preferred_element_type=jnp.float32
    )
    lowered = lax.psum(partial_low, "tensor").astype(jnp.bfloat16)
    slot_out = jnp.einsum(
        "sxcr,xrd->sxcd", lowered, trained_b, preferred_element_type=jnp.float32
    ).astype(jnp.bfloat16)
    received = lax.all_to_all(slot_out, "expert", split_axis=0, concat_axis=0, tiled=True)
    flat_rows = received.reshape(experts_all * capacity, half_width)
    total = jnp.zeros((tok_rows, half_width), jnp.float32)
    for route in range(top_count):
        picked = flat_rows[flat_index[:, route]].astype(jnp.float32)
        total = total + gate_weights[:, route, None] * picked
    adapter_out = total.astype(jnp.bfloat16)
    slot_grad = build_at_experts(
        routes, gate_weights, cotangent, local_experts, capacity, experts_all
    )
    partial_back = jnp.einsum(
        "sxcd,xrd->sxcr", slot_grad, trained_b, preferred_element_type=jnp.float32
    )
    projected = lax.psum(partial_back, "tensor").astype(jnp.bfloat16)
    grad_rows = jnp.einsum("sxcr,sxcd->xrd", lowered, slot_grad, preferred_element_type=jnp.float32)
    share_rows = grad_rows.shape[1] // lax.axis_size("dp")
    reduced = lax.psum(grad_rows, "dp")
    adapter_grad = lax.dynamic_slice_in_dim(
        reduced, lax.axis_index("dp") * share_rows, share_rows, 1
    )
    hidden_grad = jnp.einsum(
        "sxcr,xfr->xscf", projected, frozen_a, preferred_element_type=jnp.float32
    ).astype(jnp.bfloat16)
    return (adapter_out, adapter_grad, hidden_grad[:, None])


def solution(mesh):
    in_specs = (
        P(("groups", "expert"), "dp", None, None, "tensor"),
        P("expert", "tensor", None),
        P("expert", None, "tensor"),
        P(("groups", "expert", "dp"), None),
        P(("groups", "expert", "dp"), None),
        P(("groups", "expert", "dp"), "tensor"),
    )
    out_specs = (
        P(("groups", "expert", "dp"), "tensor"),
        P(("groups", "expert"), "dp", "tensor"),
        P(("groups", "expert"), "dp", None, None, "tensor"),
    )
    return jax.shard_map(local, mesh=mesh, in_specs=in_specs, out_specs=out_specs, check_vma=False)
```

profile of v0, /device:TPU:0, one launch (start us, length us, event | category | flops | bytes accessed | tf_op | source)
XLA Modules:
  0.0 304.6 jit_solution(133212238736157523)
XLA Ops:
  7.2 0.7 all-gather.2.cloned.1.call-update
  7.9 14.9 %all_gather.9 = s32[512,8]{0,1:T(8,128)S(1)} all-gather(s32[128,8]{0,1:T(8,128)} %param.9), channel_id=1, replica_groups=mesh['groups'=2,'expert'=4,'dp'=2,'tensor'=2] {'expert'}, dimensions={0}, use_global_device_ids=true | all-gather | bytes 20480 | tf_op jit(solution)/shard_map/all_gather | solution.py:19
  22.9 0.1 copy.92
  23.0 0.1 copy.93
  23.2 13.5 %all_gather.10 = f32[512,8]{0,1:T(8,128)S(1)} all-gather(f32[128,8]{0,1:T(8,128)} %param.10), channel_id=1, replica_groups=mesh['groups'=2,'expert'=4,'dp'=2,'tensor'=2] {'expert'}, dimensions={0}, use_global_device_ids=true | all-gather | bytes 20480 | tf_op jit(solution)/shard_map/all_gather | solution.py:20
  36.7 0.1 copy.98
  36.8 0.2 reshape.271
  37.0 0.1 iota_add_fusion
  37.1 0.1 reshape.279
  37.2 0.1 iota.28
  37.3 0.2 iota.29
  37.5 0.3 reduce_window_sum.23
  37.8 0.1 copy.95
  37.9 0.1 fusion.13
  38.0 0.1 reshape.261
  38.2 0.2 reshape.179
  38.4 34.4 %gather_fusion.10 = s32[4096]{0:T(1024)S(1)} fusion(s32[4,128,16]{2,1,0:T(8,128)S(1)} %sub.23, s32[4096]{0:T(1024)S(1)} %reshape.261), kind=kCustom, calls=%fused_computation.10 | custom fusion | bytes 81920 | tf_op jit(solution)/shard_map/vmap(jit(take_along_axis))/gather | solution.py:11
  72.7 0.1 compare_select_fusion.1
  72.8 15.5 %scatter_custom_fusion.1 = s32[1281]{0:T(1024)S(1)} fusion(s32[4096]{0:T(1024)S(1)} %bitcast.89, s32[4096]{0:T(1024)S(1)} %reshape.279, s32[]{:T(128)} %constant.22.clone.1), kind=kCustom, calls=%fused_computation.57 | custom fusion | bytes 5128 | tf_op jit(solution)/shard_map/scatter | solution.py:33
  88.3 15.5 %scatter_custom_fusion = f32[1281]{0:T(1024)S(1)} fusion(s32[4096]{0:T(1024)S(1)} %bitcast.90, f32[4096]{0:T(1024)S(1)} %reshape.271, f32[]{:T(128)} %constant.27.clone.1), kind=kCustom, calls=%fused_computation.59 | custom fusion | bytes 5128 | tf_op jit(solution)/shard_map/scatter | solution.py:36
  103.9 0.1 mul.158
  104.0 0.6 convolution_bitcast_fusion.1
  104.7 12.7 %gather_fusion.8 = bf16[1280,2048]{1,0:T(8,128)(2,1)} fusion(bf16[512,2048]{1,0:T(8,128)(2,1)} %all-gather.2.cloned.1.call-done, s32[2048]{0:T(1024)S(1)} %pad_clamp_fusion), kind=kCustom, calls=%fused_computation.8 | custom fusion | bytes 10490880 | tf_op jit(solution)/shard_map/gather | solution.py:38
  117.4 4.8 %fusion.5 = f32[4,4,80,64]{2,3,0,1:T(8,128)S(1)} fusion(f32[4,4,80]{2,0,1:T(4,128)S(1)} %copy.99, bf16[4,64,2048]{2,1,0:T(8,128)(2,1)S(1)} %copy-done, bf16[4,4,80,2048]{3,2,1,0:T(8,128)(2,1)} %bitcast.83), kind=kOutput, calls=%fused_computation.21 | convolution fusion | flops 343408640 | bytes 6624256 | tf_op jit(solution)/shard_map/sxcd,xrd->sxcr/dot_general | solution.py:69
  122.2 6.3 %all-reduce.5 = (bf16[4,4,80,64]{2,3,0,1:T(8,128)(2,1)S(1)}, bf16[4,4,80,64]{2,3,0,1:T(8,128)(2,1)S(1)}) all-reduce(f32[4,4,80,64]{2,3,0,1:T(8,128)S(1)} %convolution_bitcast_fusion.1, f32[4,4,80,64]{2,3,0,1:T(8,128)S(1)} %fusion.5), channel_id=1, replica_groups=mesh['groups'=2,'expert'=4,'dp'=2,'tensor'=2] {'tensor'}, use_global_device_ids=true, to_apply=%region_0.0 | all-reduce | flops 163840 | bytes 983040 | tf_op jit(solution)/shard_map/psum | solution.py:55
  128.4 1.6 convert_bitcast_fusion
  130.0 2.8 copy.87
  132.8 5.0 %all-to-all-start = ((bf16[4,4,80,2048]{3,2,1,0:T(8,128)(2,1)}), bf16[4,4,80,2048]{3,2,1,0:T(8,128)(2,1)}, u32[]{:S(2)}, u32[]{:S(2)}) async-start(bf16[4,4,80,2048]{3,2,1,0:T(8,128)(2,1)} %copy.87), calls=%async_computation | async-start | bytes 10485760 | tf_op jit(solution)/shard_map/all_to_all | solution.py:59
  137.9 5.2 %convolution_bitcast_fusion = f32[4,64,2048]{2,1,0:T(8,128)} fusion(f32[4,4,80]{2,0,1:T(4,128)S(1)} %copy.99, bf16[4,4,80,64]{2,3,0,1:T(8,128)(2,1)S(1)} %get-tuple-element.21, bf16[4,4,80,2048]{3,2,1,0:T(8,128)(2,1)} %bitcast.84), kind=kOutput, calls=%fused_computation.16 | convolution fusion | flops 343408640 | bytes 7508992 | tf_op jit(solution)/shard_map/sxcr,sxcd->xrd/dot_general | solution.py:73
  143.2 0.1 copy.88
  143.3 0.1 copy.90
  143.4 0.1 reshape.255
  143.5 0.2 reduce_window_sum.22
  143.7 7.2 %gather_fusion.9 = s32[1024]{0:T(1024)S(1)} fusion(s32[128,16]{1,0:T(8,128)S(1)} %sub.20, s32[1024]{0:T(1024)S(1)} %reshape.255), kind=kCustom, calls=%fused_computation.9 | custom fusion | bytes 16384 | tf_op jit(solution)/shard_map/jit(take_along_axis)/gather | solution.py:11
  150.9 0.1 reshape.258
  151.2 1.4 fusion.4
  152.6 55.0 %all-reduce.4.cloned.1.call-done = f32[4,64,2048]{2,1,0:T(8,128)} async-done(((f32[4,64,2048]{2,1,0:T(8,128)}), f32[4,64,2048]{2,1,0:T(8,128)}) %all-reduce.4.cloned.1.call-update) | async-done | bytes 2097168 | tf_op jit(solution)/shard_map/psum | solution.py:75
  207.6 2.3 constant_dynamic-slice_fusion
  209.9 44.4 %all-to-all-done = bf16[4,4,80,2048]{3,2,1,0:T(8,128)(2,1)} async-done(((bf16[4,4,80,2048]{3,2,1,0:T(8,128)(2,1)}), bf16[4,4,80,2048]{3,2,1,0:T(8,128)(2,1)}, u32[]{:S(2)}, u32[]{:S(2)}) %all-to-all-start) | async-done | bytes 5242912 | tf_op jit(solution)/shard_map/all_to_all | solution.py:59
  254.3 4.6 %gather_fusion.7 = bf16[128,2048]{1,0:T(8,128)(2,1)S(1)} fusion(bf16[1280,2048]{1,0:T(8,128)(2,1)} %bitcast.8, s32[1024]{0:T(1024)S(1)} %get-tuple-element.39), kind=kCustom, calls=%fused_computation.7 | custom fusion | bytes 1049088 | tf_op jit(solution)/shard_map/gather | solution.py:63
  258.9 4.6 %gather_fusion.6 = bf16[128,2048]{1,0:T(8,128)(2,1)S(1)} fusion(bf16[1280,2048]{1,0:T(8,128)(2,1)} %bitcast.8, s32[1024]{0:T(1024)S(1)} %get-tuple-element.40), kind=kCustom, calls=%fused_computation.6 | custom fusion | bytes 1049088 | tf_op jit(solution)/shard_map/gather | solution.py:63
  263.5 4.6 %gather_fusion.5 = bf16[128,2048]{1,0:T(8,128)(2,1)S(1)} fusion(bf16[1280,2048]{1,0:T(8,128)(2,1)} %bitcast.8, s32[1024]{0:T(1024)S(1)} %get-tuple-element.41), kind=kCustom, calls=%fused_computation.5 | custom fusion | bytes 1049088 | tf_op jit(solution)/shard_map/gather | solution.py:63
  268.1 4.6 %gather_fusion.4 = bf16[128,2048]{1,0:T(8,128)(2,1)S(1)} fusion(bf16[1280,2048]{1,0:T(8,128)(2,1)} %bitcast.8, s32[1024]{0:T(1024)S(1)} %get-tuple-element.42), kind=kCustom, calls=%fused_computation.4 | custom fusion | bytes 1049088 | tf_op jit(solution)/shard_map/gather | solution.py:63
  272.8 5.4 %gather_fusion.3 = bf16[128,2048]{1,0:T(8,128)(2,1)} fusion(bf16[1280,2048]{1,0:T(8,128)(2,1)} %bitcast.8, s32[1024]{0:T(1024)S(1)} %get-tuple-element.43), kind=kCustom, calls=%fused_computation.3 | custom fusion | bytes 1049088 | tf_op jit(solution)/shard_map/gather | solution.py:63
  278.2 5.4 %gather_fusion.2 = bf16[128,2048]{1,0:T(8,128)(2,1)} fusion(bf16[1280,2048]{1,0:T(8,128)(2,1)} %bitcast.8, s32[1024]{0:T(1024)S(1)} %get-tuple-element.44), kind=kCustom, calls=%fused_computation.2 | custom fusion | bytes 1049088 | tf_op jit(solution)/shard_map/gather | solution.py:63
  283.6 5.6 %gather_fusion.1 = bf16[128,2048]{1,0:T(8,128)(2,1)} fusion(bf16[1280,2048]{1,0:T(8,128)(2,1)} %bitcast.8, s32[1024]{0:T(1024)S(1)} %get-tuple-element.45), kind=kCustom, calls=%fused_computation.1 | custom fusion | bytes 1049088 | tf_op jit(solution)/shard_map/gather | solution.py:63
  289.2 5.4 %gather_fusion = bf16[128,2048]{1,0:T(8,128)(2,1)} fusion(bf16[1280,2048]{1,0:T(8,128)(2,1)} %bitcast.8, s32[1024]{0:T(1024)S(1)} %get-tuple-element.46), kind=kCustom, calls=%fused_computation | custom fusion | bytes 1049088 | tf_op jit(solution)/shard_map/gather | solution.py:63
  294.6 3.2 %add_convert_fusion = bf16[128,2048]{1,0:T(8,128)(2,1)} fusion(bf16[128,2048]{1,0:T(8,128)(2,1)S(1)} %gather_fusion.7, bf16[128,2048]{1,0:T(8,128)(2,1)S(1)} %gather_fusion.6, bf16[128,2048]{1,0:T(8,128)(2,1)S(1)} %gather_fusion.5, bf16[128,2048]{1,0:T(8,128)(2,1)S(1)} %gather_fusion.4, bf16[128,2048]{1,0:T(8,128)(2,1)} %gather_fusion.3, ...), kind=kLoop, calls=%fused_computation.24 | loop fusion | flops 6291456 | bytes 4722688 | tf_op jit(solution)/shard_map/convert_element_type | solution.py:65
  (32 shorter events, 0.4 us)
Async XLA Ops:
  7.2 110.2 %copy-start = (bf16[4,64,2048]{2,1,0:T(8,128)(2,1)S(1)}, bf16[4,64,2048]{2,1,0:T(8,128)(2,1)}, u32[]{:S(2)}) copy-start(bf16[4,64,2048]{2,1,0:T(8,128)(2,1)} %param.8) | copy-start | bytes 3145732
  7.2 97.5 %all-gather.2.cloned.1.call-start = ((), (), s32[]{:S(2)}) async-start(), calls=%async_computation.1 | async-start | bytes 2621440 | tf_op jit(solution)/shard_map/all_gather | solution.py:18
  38.3 65.6 %copy-start.1 = (bf16[4,1,4,80,384]{4,3,2,1,0:T(8,128)(2,1)S(1)}, bf16[4,1,4,80,384]{4,3,2,1,0:T(8,128)(2,1)}, u32[]{:S(2)}) copy-start(bf16[4,1,4,80,384]{4,3,2,1,0:T(8,128)(2,1)} %param.6) | copy-start | bytes 2949124
  38.4 65.6 %copy-start.2 = (bf16[4,384,64]{1,2,0:T(8,128)(2,1)S(1)}, bf16[4,384,64]{1,2,0:T(8,128)(2,1)}, u32[]{:S(2)}) copy-start(bf16[4,384,64]{1,2,0:T(8,128)(2,1)} %param.7) | copy-start | bytes 589828
  132.8 121.5 %all-to-all-start = ((bf16[4,4,80,2048]{3,2,1,0:T(8,128)(2,1)}), bf16[4,4,80,2048]{3,2,1,0:T(8,128)(2,1)}, u32[]{:S(2)}, u32[]{:S(2)}) async-start(bf16[4,4,80,2048]{3,2,1,0:T(8,128)(2,1)} %copy.87), calls=%async_computation | async-start | bytes 10485760 | tf_op jit(solution)/shard_map/all_to_all | solution.py:59
  137.8 5.3 %copy-start.3 = (s32[128,8]{0,1:T(8,128)S(1)}, s32[128,8]{0,1:T(8,128)}, u32[]{:S(2)}) copy-start(s32[128,8]{0,1:T(8,128)} %param.9) | copy-start | bytes 12292
  137.9 69.7 %all-reduce.4.cloned.1.call-start = ((), (), s32[]{:S(2)}) async-start(), calls=%async_computation.2 | async-start | bytes 4194304 | tf_op jit(solution)/shard_map/psum | solution.py:75
  143.7 7.5 %copy-start.4 = (f32[128,8]{0,1:T(8,128)S(1)}, f32[128,8]{0,1:T(8,128)}, u32[]{:S(2)}) copy-start(f32[128,8]{0,1:T(8,128)} %param.10) | copy-start | bytes 12292
Sparse Core Ops, SparseCore 0:
  9.6 48.8 all-gather.1
  143.3 64.2 all-reduce.3
where the time goes:
time: 305 us
  local copies, waits for them, and re-layouts  133 us (44%)
  waiting for transfers between devices  100 us (33%)
  blocking collectives  34.7 us (11%)
  between operations  14.4 us (5%)
  matrix products  13.6 us (4%)
  starting transfers between devices  5.12 us (2%)
  other arithmetic  4.05 us (1%)
    psum x1, waiting for transfers between devices, local(): reduced = lax.psum(grad_rows, 'dp')  55 us
    all_to_all x1, waiting for transfers between devices, local(): lax.all_to_all(slot_out, 'expert', split_axis=0, concat_axis=0, tiled=True)  44.4 us
    gather x7, local copies, waits for them, and re-layouts, route_slots(): return jnp.take_along_axis(before, routes, axis=1)  42.1 us
    gather x8, local copies, waits for them, and re-layouts, local(): picked = flat_rows[flat_index[:, route]].astype(jnp.float32)  40.2 us
    scatter x1, local copies, waits for them, and re-layouts, build_at_experts(): jnp.zeros((slot_total + 1,), jnp.float32).at[target]  15.5 us
    scatter x1, local copies, waits for them, and re-layouts, build_at_experts(): jnp.zeros((slot_total + 1,), jnp.int32).at[target].set(token_id.reshape(-1))  15.5 us
    all_gather x1, blocking collectives, build_at_experts(): all_routes = lax.all_gather(routes, 'expert', axis=0, tiled=True)  14.9 us
    all_gather x1, blocking collectives, build_at_experts(): all_gates = lax.all_gather(gate_weights, 'expert', axis=0, tiled=True)  13.5 us
  transfers between devices with their start and end apart: 3, of which 2 were waited for; matrix products, arithmetic and copies ran while one was open for 28% of the time, Pallas kernels for 0%

commit v1 on v0

v1 whole, which is shorter than its diff:
```python
import jax
import jax.numpy as jnp
from jax import lax
from jax.sharding import PartitionSpec as P


def token_tables(routes, gate_weights, experts_all):
    rows = routes.shape[0]
    ids = jnp.arange(experts_all, dtype=jnp.int32)
    match = routes.T[:, None, :] == ids[None, :, None]
    gates = jnp.sum(jnp.where(match, gate_weights.T[:, None, :], 0.0), axis=0)
    hits = jnp.any(match, axis=0)
    upper = jnp.triu(jnp.ones((rows, rows), jnp.bfloat16), 1)
    before = jnp.dot(hits.astype(jnp.bfloat16), upper, preferred_element_type=jnp.float32)
    return jnp.stack([jnp.where(hits, before, -1.0), gates])


def local(hidden, frozen_a, trained_b, routes, gate_weights, cotangent):
    f32, bf16 = jnp.float32, jnp.bfloat16
    n_local, _, rank = frozen_a.shape
    blocks = lax.axis_size("expert")
    capacity = hidden.shape[3]
    rows = routes.shape[0]
    tables = token_tables(routes, gate_weights, n_local * blocks)
    tables = lax.all_gather(tables, "expert", axis=0)
    all_cot = lax.all_gather(cotangent, "expert", axis=0)
    tables = lax.dynamic_slice_in_dim(tables, lax.axis_index("expert") * n_local, n_local, 2)
    places, gates = tables[:, 0], tables[:, 1]
    pick = (places[..., None] == jnp.arange(capacity, dtype=f32)).astype(bf16)
    part = jnp.einsum("xscf,xfr->sxcr", hidden[:, 0], frozen_a, preferred_element_type=f32)
    lowered = lax.psum(part, "tensor").astype(bf16)
    low_tok = jnp.einsum("sxtc,sxcr->sxtr", pick, lowered, preferred_element_type=f32)
    low_tok = (low_tok * gates[..., None]).astype(bf16)
    low_tok = low_tok.transpose(0, 2, 1, 3).reshape(blocks, rows, n_local * rank)
    up = trained_b.reshape(n_local * rank, -1)
    out_part = jnp.einsum("str,rd->std", low_tok, up, preferred_element_type=f32).astype(bf16)
    got = lax.all_to_all(out_part, "expert", split_axis=0, concat_axis=0, tiled=True)
    adapter_out = jnp.sum(got.astype(f32), axis=0).astype(bf16)
    back = jnp.einsum("std,rd->str", all_cot, up, preferred_element_type=f32)
    back = lax.psum(back, "tensor").reshape(blocks, rows, n_local, rank)
    back = (back.transpose(0, 2, 1, 3) * gates[..., None]).astype(bf16)
    projected = jnp.einsum("sxtc,sxtr->sxcr", pick, back, preferred_element_type=f32).astype(bf16)
    hidden_grad = jnp.einsum(
        "sxcr,xfr->xscf", projected, frozen_a, preferred_element_type=f32
    ).astype(bf16)
    grad = jnp.einsum("str,std->rd", low_tok, all_cot, preferred_element_type=f32)
    grad = grad.reshape(n_local, rank, -1)
    adapter_grad = lax.psum_scatter(grad, "dp", scatter_dimension=1, tiled=True)
    return adapter_out, adapter_grad, hidden_grad[:, None]


def solution(mesh):
    in_specs = (
        P(("groups", "expert"), "dp", None, None, "tensor"),
        P("expert", "tensor", None),
        P("expert", None, "tensor"),
        P(("groups", "expert", "dp"), None),
        P(("groups", "expert", "dp"), None),
        P(("groups", "expert", "dp"), "tensor"),
    )
    out_specs = (
        P(("groups", "expert", "dp"), "tensor"),
        P(("groups", "expert"), "dp", "tensor"),
        P(("groups", "expert"), "dp", None, None, "tensor"),
    )
    return jax.shard_map(local, mesh=mesh, in_specs=in_specs, out_specs=out_specs, check_vma=False)
```

time: 305 us -> 128 us (0.42)
  local copies, waits for them, and re-layouts: 133 us -> 0.05 us
  waiting for transfers between devices: 100 us -> 29 us
  blocking collectives: 34.7 us -> 71.2 us
  starting transfers between devices: 5.12 us -> 0.12 us
    gather x16 -> x0, local copies, waits for them, and re-layouts: 95 us -> none  [the longest x7 42.1 us: route_slots(): return jnp.take_along_axis(before, routes, axis=1)]
    psum x1, waiting for transfers between devices: 55 us -> 0.01 us  [local(): back = lax.psum(back, 'tensor').reshape(blocks, rows, n_local, rank)]
    all_to_all x0 -> x1, blocking collectives: none -> 50.9 us  [local(): lax.all_to_all(out_part, 'expert', split_axis=0, concat_axis=0, tiled=True)]
    all_to_all x1 -> x0, waiting for transfers between devices: 44.4 us -> none  [local(): lax.all_to_all(slot_out, 'expert', split_axis=0, concat_axis=0, tiled=True)]
    scatter x2 -> x0, local copies, waits for them, and re-layouts: 31 us -> none  [the longest x1 15.5 us: build_at_experts(): jnp.zeros((slot_total + 1,), jnp.float32).at[target]]
    all_gather x1, waiting for transfers between devices: 0.02 us -> 28.3 us  [local(): all_cot = lax.all_gather(cotangent, 'expert', axis=0)]
    all_gather x2 -> x1, blocking collectives: 28.5 us -> 14.9 us  [local(): tables = lax.all_gather(tables, 'expert', axis=0)]
    all_to_all x1 -> x0, starting transfers between devices: 5.04 us -> none  [local(): lax.all_to_all(slot_out, 'expert', split_axis=0, concat_axis=0, tiled=True)]
  transfers between devices with their start and end apart: 3 -> 3, of which waited for: 2 -> 1; matrix products, arithmetic and copies ran while one was open for 28% -> 8% of each run, Pallas kernels for 0% -> 0%
where the time goes in v1:
time: 128 us
  blocking collectives  71.2 us (56%)
  waiting for transfers between devices  29 us (23%)
  between operations  13.9 us (11%)
  matrix products  12 us (9%)
  other arithmetic  1.35 us (1%)
    all_to_all x1, blocking collectives, local(): lax.all_to_all(out_part, 'expert', split_axis=0, concat_axis=0, tiled=True)  50.9 us
    all_gather x1, waiting for transfers between devices, local(): all_cot = lax.all_gather(cotangent, 'expert', axis=0)  28.3 us
    all_gather x1, blocking collectives, local(): tables = lax.all_gather(tables, 'expert', axis=0)  14.9 us
    psum x1, blocking collectives, local(): lowered = lax.psum(part, 'tensor').astype(bf16)  5.31 us
    dot_general x1, matrix products, local(): back = jnp.einsum('std,rd->str', all_cot, up, preferred_element_type=f32)  3.28 us
    dot_general x1, matrix products, local(): jnp.einsum('sxcr,xfr->xscf', projected, frozen_a, preferred_element_type=...  2.65 us
  transfers between devices with their start and end apart: 3, of which 1 were waited for; matrix products, arithmetic and copies ran while one was open for 8% of the time, Pallas kernels for 0%

profile of v1, /device:TPU:0, one launch (start us, length us, event | category | flops | bytes accessed | tf_op | source)
XLA Modules:
  0.0 127.5 jit_solution(812364529948045776)
XLA Ops:
  7.2 0.0 copy-start
  7.2 0.0 copy-start.3
  7.2 0.0 copy-start.4
  7.2 0.0 all-gather.4.cloned.1.call-start
  7.2 0.7 all-gather.4.cloned.1.call-update
  7.9 0.0 all-reduce.3.cloned.1.call-start
  8.0 2.0 %convolution_bitcast_fusion.2 = f32[4,4,80,64]{2,3,1,0:T(8,128)S(1)} fusion(bf16[4,384,64]{1,2,0:T(8,128)(2,1)} %param.7, bf16[4,1,4,80,384]{4,3,2,1,0:T(8,128)(2,1)} %param.6), kind=kOutput, calls=%fused_computation.5 | convolution fusion | flops 62914560 | bytes 1507328 | tf_op jit(solution)/shard_map/xscf,xfr->sxcr/dot_general | solution.py:30
  9.9 0.0 copy-done.3
  10.0 0.1 fusion.3
  10.1 0.0 copy-done.4
  10.1 14.9 %all-gather = f32[8,16,128]{2,1,0:T(8,128)S(1)} all-gather(f32[2,16,128]{2,1,0:T(8,128)S(1)} %pad_maximum_fusion), channel_id=2, replica_groups=mesh['groups'=2,'expert'=4,'dp'=2,'tensor'=2] {'expert'}, dimensions={0}, use_global_device_ids=true | all-gather | bytes 81920 | tf_op jit(solution)/shard_map/all_gather | solution.py:25
  25.1 5.3 %all-reduce.4 = bf16[4,4,80,64]{2,3,1,0:T(8,128)(2,1)} all-reduce(f32[4,4,80,64]{2,3,1,0:T(8,128)S(1)} %convolution_bitcast_fusion.2), channel_id=1, replica_groups=mesh['groups'=2,'expert'=4,'dp'=2,'tensor'=2] {'tensor'}, use_global_device_ids=true, to_apply=%region_2.3 | all-reduce | flops 81920 | bytes 491520 | tf_op jit(solution)/shard_map/psum | solution.py:31
  30.4 28.3 %all-gather.4.cloned.1.call-done = bf16[512,2048]{1,0:T(8,128)(2,1)} async-done(((bf16[128,2048]{1,0:T(8,128)(2,1)}), bf16[512,2048]{1,0:T(8,128)(2,1)}) %all-gather.4.cloned.1.call-update) | async-done | bytes 2097168 | tf_op jit(solution)/shard_map/all_gather | solution.py:26
  58.7 0.0 copy-done
  58.7 0.0 copy-start.1
  58.7 3.3 %fusion.20 = f32[4,128,256]{1,2,0:T(8,128)} fusion(bf16[4,128,2048]{2,1,0:T(8,128)(2,1)} %bitcast.74, bf16[256,2048,1]{1,0,2:T(8,128)(2,1)S(1)} %bitcast.73), kind=kOutput, calls=%fused_computation.34 | convolution fusion | flops 536870912 | bytes 3670016 | tf_op jit(solution)/shard_map/std,rd->str/dot_general | solution.py:39
  62.0 0.0 all-reduce.3.cloned.1.call-update
  62.0 0.0 reduce-scatter.2.cloned.1.call-start
  62.1 1.2 fusion.2
  63.3 0.0 copy-done.1
  63.3 2.1 %convolution_bitcast_fusion = f32[4,64,2048]{2,1,0:T(8,128)} fusion(bf16[4,128,2048,1]{2,1,3,0:T(8,128)(2,1)S(1)} %bitcast.75, bf16[4,128,4,64]{1,3,2,0:T(8,128)(2,1)S(1)} %fusion.2), kind=kOutput, calls=%fused_computation.1 | convolution fusion | flops 536870912 | bytes 4456448 | tf_op jit(solution)/shard_map/str,std->rd/dot_general | solution.py:46
  65.4 0.0 reduce-scatter.2.cloned.1.call-update
  65.4 0.7 bitcast_convert_fusion
  66.1 50.9 %all_to_all.5 = bf16[4,128,2048]{2,1,0:T(8,128)(2,1)S(1)} all-to-all(bf16[4,128,2048]{2,1,0:T(8,128)(2,1)S(1)} %bitcast_convert_fusion), channel_id=1, replica_groups=mesh['groups'=2,'expert'=4,'dp'=2,'tensor'=2] {'expert'}, dimensions={0} | all-to-all | bytes 4194304 | tf_op jit(solution)/shard_map/all_to_all | solution.py:37
  117.0 0.0 copy-start.2
  117.0 1.3 %reduce_sum.22 = bf16[128,2048]{1,0:T(8,128)(2,1)} reduce(bf16[4,128,2048]{2,1,0:T(8,128)(2,1)S(1)} %all_to_all.5, bf16[]{:T(256)} %constant.5.clone.1), dimensions={0}, to_apply=%region_3.4 | reduce | flops 786432 | bytes 2621442 | tf_op jit(solution)/shard_map/reduce_sum | solution.py:38
  118.3 0.0 all-reduce.3.cloned.1.call-done
  118.3 0.0 copy-done.2
  118.3 2.7 %fusion = bf16[4,1,4,80,384]{4,3,2,1,0:T(8,128)(2,1)} fusion(bf16[4,384,64]{1,2,0:T(8,128)(2,1)S(1)} %copy-done.2, f32[4,4,128]{2,0,1:T(4,128)S(1)} %copy.22, f32[4,4,128,64]{2,3,1,0:T(8,128)} %all-reduce.3.cloned.1.call-done, f32[4,4,128]{2,1,0:T(4,128)S(1)} %get-tuple-element.15), kind=kOutput, calls=%fused_computation.3 | convolution fusion | flops 84885504 | bytes 1720320 | tf_op jit(solution)/shard_map/sxcr,xfr->xscf/dot_general | solution.py:43
  121.0 0.0 reduce-scatter.2.cloned.1.call-done
  (5 shorter events, 0.1 us)
Async XLA Ops:
  7.2 51.5 %copy-start = (bf16[4,64,2048]{2,1,0:T(8,128)(2,1)S(1)}, bf16[4,64,2048]{2,1,0:T(8,128)(2,1)}, u32[]{:S(2)}) copy-start(bf16[4,64,2048]{2,1,0:T(8,128)(2,1)} %param.8) | copy-start | bytes 3145732
  7.2 2.8 %copy-start.3 = (s32[128,8]{0,1:T(8,128)S(1)}, s32[128,8]{0,1:T(8,128)}, u32[]{:S(2)}) copy-start(s32[128,8]{0,1:T(8,128)} %param.9) | copy-start | bytes 12292
  7.2 2.9 %copy-start.4 = (f32[128,8]{0,1:T(8,128)S(1)}, f32[128,8]{0,1:T(8,128)}, u32[]{:S(2)}) copy-start(f32[128,8]{0,1:T(8,128)} %param.10) | copy-start | bytes 12292
  7.2 51.5 %all-gather.4.cloned.1.call-start = ((), (), s32[]{:S(2)}) async-start(), calls=%async_computation.4 | async-start | bytes 2621440 | tf_op jit(solution)/shard_map/all_gather | solution.py:26
  7.9 110.4 %all-reduce.3.cloned.1.call-start = ((), (), s32[]{:S(2)}) async-start(), calls=%async_computation.3 | async-start | bytes 1048576 | tf_op jit(solution)/shard_map/psum | solution.py:40
  58.7 4.6 %copy-start.1 = (bf16[512,2048]{1,0:T(8,128)(2,1)S(1)}, bf16[512,2048]{1,0:T(8,128)(2,1)}, u32[]{:S(2)}) copy-start(bf16[512,2048]{1,0:T(8,128)(2,1)} %all-gather.4.cloned.1.call-done) | copy-start | bytes 6291460
  62.0 59.0 %reduce-scatter.2.cloned.1.call-start = ((), (), s32[]{:S(2)}) async-start(), calls=%async_computation.2 | async-start | bytes 3145728 | tf_op jit(solution)/shard_map/reduce_scatter | solution.py:48
  117.0 1.3 %copy-start.2 = (bf16[4,384,64]{1,2,0:T(8,128)(2,1)S(1)}, bf16[4,384,64]{1,2,0:T(8,128)(2,1)}, u32[]{:S(2)}) copy-start(bf16[4,384,64]{1,2,0:T(8,128)(2,1)} %param.7) | copy-start | bytes 589828
Sparse Core Ops, SparseCore 0:
  9.6 49.0 all-gather.3
  62.1 17.5 all-reduce.2
  82.6 33.0 reduce-scatter.1

commit v2 on v1

v2 whole, which is shorter than its diff:
```python
import functools

import jax
import jax.numpy as jnp
from jax import lax
from jax.experimental import pallas as pl
from jax.experimental.pallas import tpu as pltpu
from jax.sharding import PartitionSpec as P

F32, BF16 = jnp.float32, jnp.bfloat16
MESH = pl.DeviceIdType.MESH
PARTS = 4


def nt_dot(a, b):
    return lax.dot_general(a, b, (((1,), (1,)), ((), ())), preferred_element_type=F32)


def token_tables(routes, gate_weights, experts_all, n_local):
    rows = routes.shape[0]
    ids = jnp.arange(experts_all, dtype=jnp.int32)
    match = routes.T[:, None, :] == ids[None, :, None]
    gates = jnp.sum(jnp.where(match, gate_weights.T[:, None, :], 0.0), axis=0)
    hits = jnp.any(match, axis=0)
    upper = jnp.triu(jnp.ones((rows, rows), BF16), 1)
    before = jnp.dot(hits.astype(BF16), upper, preferred_element_type=F32)
    places = jnp.where(hits, before, -1.0).reshape(-1, n_local, rows)
    return jnp.concatenate([places, gates.reshape(-1, n_local, rows)], axis=1)


def kernel(
    dims, hidden, frozen, up, tables, cot, out, grad, hgrad,
    cot_buf, right_sum, left_sum, tab_buf, low_mine, low_other, pick, low_tr, low_tok,
    back_mine, back_other, grad_out_buf, grad_in_buf,
    tab_send, tab_recv, pair_send, pair_recv,
    fwd_r_send, fwd_l_send, fwd_recv, sum_r_send, sum_l_send, sum_r_recv, sum_l_recv,
    dp_send, dp_recv,
):
    n, n_dp, n_local, rank, cap, rows = dims
    width = up.shape[1]
    part = width // PARTS
    share = rank // n_dp
    me, my_dp, core = lax.axis_index("expert"), lax.axis_index("dp"), lax.axis_index("tensor")
    has_right, has_left = me < n - 1, me > 0

    def cols(q):
        return pl.ds(q * part, part)

    def remote(src, dst, send, recv, where):
        return pltpu.make_async_remote_copy(
            src_ref=src, dst_ref=dst, send_sem=send, recv_sem=recv,
            device_id=where, device_id_type=MESH,
        )

    def fwd_right(q, b):
        block = cot_buf.at[q, b]
        return remote(block, block, fwd_r_send.at[q, b], fwd_recv.at[q, b], {"expert": me + 1})

    def fwd_left(q, b):
        block = cot_buf.at[q, b]
        return remote(block, block, fwd_l_send.at[q, b], fwd_recv.at[q, b], {"expert": me - 1})

    def sum_right(q, j):
        block = right_sum.at[q, j]
        return remote(block, block, sum_r_send.at[q, j], sum_r_recv.at[q, j], {"expert": me + 1})

    def sum_left(q, j):
        block = left_sum.at[q, j]
        return remote(block, block, sum_l_send.at[q, j], sum_l_recv.at[q, j], {"expert": me - 1})

    def tab_copy(k):
        j = lax.rem(me + k, n)
        return remote(tables.at[j], tab_buf.at[me], tab_send.at[k], tab_recv.at[me], {"expert": j})

    def dp_copy(q, d):
        return remote(
            grad_out_buf.at[q, d], grad_in_buf.at[q, my_dp],
            dp_send.at[q, d], dp_recv.at[q, my_dp], {"dp": d},
        )

    def dp_arrival(q, d):
        return remote(
            grad_out_buf.at[q, d], grad_in_buf.at[q, d],
            dp_send.at[q, d], dp_recv.at[q, d], {"dp": d},
        )

    barrier = pltpu.get_barrier_semaphore()
    for k in range(1, n):
        pl.semaphore_signal(
            barrier, inc=1, device_id={"expert": lax.rem(me + k, n)}, device_id_type=MESH
        )
    for k in range(1, n_dp):
        pl.semaphore_signal(
            barrier, inc=1, device_id={"dp": lax.rem(my_dp + k, n_dp)}, device_id_type=MESH
        )
    pl.semaphore_signal(barrier, inc=1, device_id={"tensor": 1 - core}, device_id_type=MESH)
    for q in range(PARTS):
        cot_buf[q, me] = cot[:, q * part : (q + 1) * part]
    tab_buf[me] = tables[me]
    pl.semaphore_wait(barrier, n + n_dp - 1)

    for k in range(1, n):
        tab_copy(k).start()
    for q in range(PARTS):
        @pl.when(has_right)
        def _():
            fwd_right(q, me).start()

        @pl.when(has_left)
        def _():
            fwd_left(q, me).start()

    for x in range(n_local):
        low_mine[x * rank : (x + 1) * rank, :] = lax.dot_general(
            frozen[x], hidden[x], (((0,), (1,)), ((), ())), preferred_element_type=F32
        )
    low_copy = remote(
        low_mine, low_other, pair_send.at[0], pair_recv.at[0], {"tensor": 1 - core}
    )
    low_copy.start()

    for k in range(1, n):
        j = lax.rem(me + k, n)
        remote(
            tables.at[j], tab_buf.at[j], tab_send.at[k], tab_recv.at[j], {"expert": j}
        ).wait_recv()
    slots = lax.broadcasted_iota(jnp.int32, (n * cap, rows), 0).astype(F32)
    for b in range(n):
        tab = tab_buf[b]
        for x in range(n_local):
            want = jnp.where(tab[x : x + 1] >= 0, tab[x : x + 1] + b * cap, -1.0)
            pick[x, :, b * rows : (b + 1) * rows] = jnp.where(slots == want, 1.0, 0.0).astype(BF16)
    low_copy.wait_recv()
    for x in range(n_local):
        span = slice(x * rank, (x + 1) * rank)
        low = (low_mine[span, :] + low_other[span, :]).astype(BF16)
        for b in range(n):
            there = slice(b * rows, (b + 1) * rows)
            chosen = jnp.dot(low, pick[x, :, there], preferred_element_type=F32)
            gated = chosen * tab_buf[b, n_local + x : n_local + x + 1, :]
            low_tr[span, there] = gated
    for b in range(n):
        low_tok[b] = low_tr[:, b * rows : (b + 1) * rows].T.astype(BF16)

    def term(q, j):
        return jnp.dot(low_tok[j], up[:, cols(q)], preferred_element_type=F32)

    def finish_out(q):
        total = term(q, me)
        out_cols = cols(q)

        @pl.when(has_left)
        def _():
            sum_right(q, me).wait_recv()

        @pl.when(jnp.logical_not(has_left))
        def _():
            right_sum[q, me] = jnp.zeros((rows, part), BF16)

        @pl.when(has_right)
        def _():
            sum_left(q, me).wait_recv()

        @pl.when(jnp.logical_not(has_right))
        def _():
            left_sum[q, me] = jnp.zeros((rows, part), BF16)

        total = total + right_sum[q, me].astype(F32) + left_sum[q, me].astype(F32)
        out[:, out_cols] = total.astype(BF16)

    def finish_grad(q):
        for k in range(1, n_dp):
            d = lax.rem(my_dp + k, n_dp)
            dp_arrival(q, d).wait_recv()
            grad[:, cols(q)] += grad_in_buf[q, d].astype(F32)

    for q in range(PARTS):

        def slot(u, carry, q=q):
            from_left = u <= me
            from_right = u <= n - 1 - me
            left_block, right_block = jnp.maximum(me - u, 0), jnp.minimum(me + u, n - 1)

            @pl.when(from_left)
            def _():
                fwd_right(q, left_block).wait_recv()

                @pl.when(has_right)
                def _():
                    fwd_right(q, left_block).start()

            @pl.when(from_right)
            def _():
                fwd_left(q, right_block).wait_recv()

                @pl.when(has_left)
                def _():
                    fwd_left(q, right_block).start()

            @pl.when(jnp.logical_and(u > me, has_right))
            def _():
                j = n + me - u
                mine = term(q, j)

                @pl.when(has_left)
                def _():
                    sum_right(q, j).wait_recv()
                    right_sum[q, j] = (mine + right_sum[q, j].astype(F32)).astype(BF16)

                @pl.when(jnp.logical_not(has_left))
                def _():
                    right_sum[q, j] = mine.astype(BF16)

                sum_right(q, j).start()

            @pl.when(jnp.logical_and(u > n - 1 - me, has_left))
            def _():
                j = u - n + me
                mine = term(q, j)

                @pl.when(has_right)
                def _():
                    sum_left(q, j).wait_recv()
                    left_sum[q, j] = (mine + left_sum[q, j].astype(F32)).astype(BF16)

                @pl.when(jnp.logical_not(has_right))
                def _():
                    left_sum[q, j] = mine.astype(BF16)

                sum_left(q, j).start()

            return carry

        lax.fori_loop(1, n, slot, 0)

        cots = cot_buf[q].reshape(n * rows, part)
        back = nt_dot(up[:, cols(q)], cots)
        if q == 0:
            back_mine[...] = back
        else:
            back_mine[...] += back
        if q == PARTS - 1:
            back_copy = remote(
                back_mine, back_other, pair_send.at[1], pair_recv.at[1], {"tensor": 1 - core}
            )
            back_copy.start()
        full = jnp.dot(low_tr[...].astype(BF16), cots, preferred_element_type=F32)
        full = full.reshape(n_local, rank, part)
        for d in range(n_dp):
            piece = full[:, d * share : (d + 1) * share].reshape(n_local * share, part)

            @pl.when(my_dp == d)
            def _():
                grad[:, cols(q)] = piece

            @pl.when(my_dp != d)
            def _():
                grad_out_buf[q, d] = piece.astype(BF16)
                dp_copy(q, d).start()

        if q > 0:
            finish_out(q - 1)
            finish_grad(q - 1)

    finish_out(PARTS - 1)
    back_copy.wait_recv()
    for x in range(n_local):
        span = slice(x * rank, (x + 1) * rank)
        projected = jnp.zeros((n * cap, rank), F32)
        for b in range(n):
            there = slice(b * rows, (b + 1) * rows)
            both = back_mine[span, there] + back_other[span, there]
            both = (both * tab_buf[b, n_local + x : n_local + x + 1, :]).astype(BF16)
            projected = projected + nt_dot(pick[x, :, there], both)
        hgrad[x] = nt_dot(projected.astype(BF16), frozen[x]).astype(BF16)
    finish_grad(PARTS - 1)

    low_copy.wait_send()
    back_copy.wait_send()
    for k in range(1, n):
        tab_copy(k).wait_send()
    for q in range(PARTS):
        for k in range(1, n_dp):
            dp_copy(q, lax.rem(my_dp + k, n_dp)).wait_send()

        def drain(b, carry, q=q):
            @pl.when(jnp.logical_and(b <= me, has_right))
            def _():
                fwd_right(q, b).wait_send()

            @pl.when(jnp.logical_and(b >= me, has_left))
            def _():
                fwd_left(q, b).wait_send()

            @pl.when(b > me)
            def _():
                sum_right(q, b).wait_send()

            @pl.when(b < me)
            def _():
                sum_left(q, b).wait_send()

            return carry

        lax.fori_loop(0, n, drain, 0)


def local(hidden, frozen_a, trained_b, routes, gate_weights, cotangent):
    n_local, half_ff, rank = frozen_a.shape
    n, n_dp = lax.axis_size("expert"), lax.axis_size("dp")
    cap = hidden.shape[3]
    rows, width = cotangent.shape
    share = rank // n_dp
    part = width // PARTS
    ranks = n_local * rank
    tables = token_tables(routes, gate_weights, n_local * n, n_local)
    vmem = pl.BlockSpec(memory_space=pltpu.VMEM)
    dma = pltpu.SemaphoreType.DMA
    grid_sem = dma((PARTS, n))
    out, grad, hgrad = pl.pallas_call(
        functools.partial(kernel, (n, n_dp, n_local, rank, cap, rows)),
        out_shape=(
            jax.ShapeDtypeStruct((rows, width), BF16),
            jax.ShapeDtypeStruct((n_local * share, width), F32),
            jax.ShapeDtypeStruct((n_local, n * cap, half_ff), BF16),
        ),
        in_specs=[vmem] * 5,
        out_specs=(vmem,) * 3,
        scratch_shapes=[
            pltpu.VMEM((PARTS, n, rows, part), BF16),
            pltpu.VMEM((PARTS, n, rows, part), BF16),
            pltpu.VMEM((PARTS, n, rows, part), BF16),
            pltpu.VMEM((n, 2 * n_local, rows), F32),
            pltpu.VMEM((ranks, n * cap), F32),
            pltpu.VMEM((ranks, n * cap), F32),
            pltpu.VMEM((n_local, n * cap, n * rows), BF16),
            pltpu.VMEM((ranks, n * rows), F32),
            pltpu.VMEM((n, rows, ranks), BF16),
            pltpu.VMEM((ranks, n * rows), F32),
            pltpu.VMEM((ranks, n * rows), F32),
            pltpu.VMEM((PARTS, n_dp, n_local * share, part), BF16),
            pltpu.VMEM((PARTS, n_dp, n_local * share, part), BF16),
            dma((n,)), dma((n,)), dma((2,)), dma((2,)),
            grid_sem, grid_sem, grid_sem, grid_sem, grid_sem, grid_sem, grid_sem,
            dma((PARTS, n_dp)), dma((PARTS, n_dp)),
        ],
        compiler_params=pltpu.CompilerParams(
            collective_id=0, has_side_effects=True, vmem_limit_bytes=60 * 1024 * 1024
        ),
        cost_estimate=pl.CostEstimate(
            flops=2 * 6 * n * rows * ranks * width // 2, bytes_accessed=8 << 20, transcendentals=0
        ),
    )(
        hidden.reshape(n_local, n * cap, half_ff),
        frozen_a,
        trained_b.reshape(ranks, width),
        tables,
        cotangent,
    )
    return (
        out,
        grad.reshape(n_local, share, width),
        hgrad.reshape(n_local, 1, n, cap, half_ff),
    )


def solution(mesh):
    in_specs = (
        P(("groups", "expert"), "dp", None, None, "tensor"),
        P("expert", "tensor", None),
        P("expert", None, "tensor"),
        P(("groups", "expert", "dp"), None),
        P(("groups", "expert", "dp"), None),
        P(("groups", "expert", "dp"), "tensor"),
    )
    out_specs = (
        P(("groups", "expert", "dp"), "tensor"),
        P(("groups", "expert"), "dp", "tensor"),
        P(("groups", "expert"), "dp", None, None, "tensor"),
    )
    return jax.shard_map(local, mesh=mesh, in_specs=in_specs, out_specs=out_specs, check_vma=False)
```

time: 128 us -> 78.9 us (0.62)
  blocking collectives: 71.2 us -> 0 us
  Pallas kernels: 0 us -> 69.6 us
  waiting for transfers between devices: 29 us -> 0 us
  between operations: 13.9 us -> 0.67 us
  matrix products: 12 us -> 0.13 us
  local copies, waits for them, and re-layouts: 0.05 us -> 7.58 us
    pallas_call x0 -> x1, Pallas kernels: none -> 69.6 us  [local(): pl.pallas_call(functools.partial(kernel, (n, n_dp, n_local, rank, cap, ro...]
    all_to_all x1 -> x0, blocking collectives: 50.9 us -> none  [local(): lax.all_to_all(out_part, 'expert', split_axis=0, concat_axis=0, tiled=True)]
    all_gather x1 -> x0, waiting for transfers between devices: 28.3 us -> none  [local(): all_cot = lax.all_gather(cotangent, 'expert', axis=0)]
    all_gather x1 -> x0, blocking collectives: 14.9 us -> none  [local(): tables = lax.all_gather(tables, 'expert', axis=0)]
    dot_general x7 -> x1, matrix products: 12 us -> 0.13 us  [token_tables(): before = jnp.dot(hits.astype(BF16), upper, preferred_element_type=F32)]
    unnamed x10 -> x12, local copies, waits for them, and re-layouts: 0.03 us -> 7.58 us
    psum x1 -> x0, blocking collectives: 5.31 us -> none  [local(): lowered = lax.psum(part, 'tensor').astype(bf16)]
    reduce_sum x1 -> x0, other arithmetic: 1.31 us -> none  [local(): adapter_out = jnp.sum(got.astype(f32), axis=0).astype(bf16)]
  transfers between devices with their start and end apart: 3 -> 0, of which waited for: 1 -> 0; matrix products, arithmetic and copies ran while one was open for 8% -> 0% of each run, Pallas kernels for 0% -> 0%
where the time goes in v2:
time: 78.9 us; the launch traced here: 78.6 us
  Pallas kernels  69.6 us (88%)
  local copies, waits for them, and re-layouts  7.58 us (10%)
    pallas_call x1, Pallas kernels, local(): pl.pallas_call(functools.partial(kernel, (n, n_dp, n_local, rank, cap, ro...  69.6 us
    unnamed x12, local copies, waits for them, and re-layouts  7.58 us

profile of v2, /device:TPU:0, one launch (start us, length us, event | category | flops | bytes accessed | tf_op | source)
XLA Modules:
  0.0 78.6 jit_solution(15607349871711720814)
XLA Ops:
  0.6 0.0 copy-start.2
  0.6 0.7 copy-done.2
  1.3 0.0 copy-start.3
  1.3 0.1 convolution_select_fusion
  1.5 0.5 copy-done.3
  2.0 0.6 pad_maximum_fusion.tables
  2.7 1.8 %copy.11.frozen = bf16[4,384,64]{2,1,0:T(8,128)(2,1)} copy(bf16[4,384,64]{1,2,0:T(8,128)(2,1)} %param.7) | data formatting | bytes 393216 | tf_op args[1]
  4.5 69.6 %shard_map.85 = (bf16[128,2048]{1,0:T(8,128)(2,1)}, f32[128,2048]{1,0:T(8,128)}, bf16[4,320,384]{2,1,0:T(8,128)(2,1)}) custom-call(bf16[4,320,384]{2,1,0:T(8,128)(2,1)} %bitcast.19, bf16[4,384,64]{2,1,0:T(8,128)(2,1)} %copy.11.frozen, bf16[256,2048]{1,0:T(8,128)(2,1)} %bitcast.18, f32[4,8,128]{2,1,0:T(8,128)} %pad_maximum_fusion.tables, bf16[128,2048]{1,0:T(8,128)(2,1)} %cot.1), custom_call_target="tpu_custom_call" | custom-call | flops 1610612736 | bytes 8388608 | tf_op jit(solution)/shard_map/pallas_call | solution.py:320
  74.1 0.0 copy-start
  74.1 2.0 %copy.16 = bf16[128,2048]{1,0:T(8,128)(2,1)} copy(bf16[128,2048]{1,0:T(8,128)(2,1)} %get-tuple-element.18) | data formatting | bytes 1048576
  76.1 0.0 copy-done
  76.1 0.0 copy-start.1
  76.1 1.0 %copy.17 = f32[4,32,2048]{2,1,0:T(8,128)} copy(f32[4,32,2048]{2,1,0:T(8,128)S(1)} %bitcast.11) | data formatting | bytes 2097152
  77.0 0.6 copy-done.1
  77.6 0.9 %copy.18 = bf16[4,1,4,80,384]{4,3,2,1,0:T(8,128)(2,1)} copy(bf16[4,1,4,80,384]{4,3,2,1,0:T(8,128)(2,1)S(1)} %bitcast.12) | data formatting | bytes 1966080
  (2 shorter events, 0.0 us)
Async XLA Ops:
  0.6 0.7 copy-start.2
  1.3 0.7 copy-start.3
  74.1 2.0 %copy-start = (f32[128,2048]{1,0:T(8,128)S(1)}, f32[128,2048]{1,0:T(8,128)}, u32[]{:S(2)}) copy-start(f32[128,2048]{1,0:T(8,128)} %get-tuple-element.7) | copy-start | bytes 3145732
  76.1 1.6 %copy-start.1 = (bf16[4,320,384]{2,1,0:T(8,128)(2,1)S(1)}, bf16[4,320,384]{2,1,0:T(8,128)(2,1)}, u32[]{:S(2)}) copy-start(bf16[4,320,384]{2,1,0:T(8,128)(2,1)} %get-tuple-element.8) | copy-start | bytes 2949124

commit v3 on v2

--- a/solution.py
+++ b/solution.py
@@ -44,7 +44,7 @@
     has_right, has_left = me < n - 1, me > 0
 
     def cols(q):
-        return pl.ds(q * part, part)
+        return pl.ds(pl.multiple_of(q * part, part), part)
 
     def remote(src, dst, send, recv, where):
         return pltpu.make_async_remote_copy(
@@ -111,9 +111,7 @@
             fwd_left(q, me).start()
 
     for x in range(n_local):
-        low_mine[x * rank : (x + 1) * rank, :] = lax.dot_general(
-            frozen[x], hidden[x], (((0,), (1,)), ((), ())), preferred_element_type=F32
-        )
+        low_mine[x * rank : (x + 1) * rank, :] = nt_dot(frozen[x], hidden[x])
     low_copy = remote(
         low_mine, low_other, pair_send.at[0], pair_recv.at[0], {"tensor": 1 - core}
     )
@@ -174,76 +172,71 @@
             dp_arrival(q, d).wait_recv()
             grad[:, cols(q)] += grad_in_buf[q, d].astype(F32)
 
-    for q in range(PARTS):
-
-        def slot(u, carry, q=q):
-            from_left = u <= me
-            from_right = u <= n - 1 - me
-            left_block, right_block = jnp.maximum(me - u, 0), jnp.minimum(me + u, n - 1)
-
-            @pl.when(from_left)
-            def _():
-                fwd_right(q, left_block).wait_recv()
-
-                @pl.when(has_right)
-                def _():
-                    fwd_right(q, left_block).start()
-
-            @pl.when(from_right)
-            def _():
-                fwd_left(q, right_block).wait_recv()
-
-                @pl.when(has_left)
-                def _():
-                    fwd_left(q, right_block).start()
-
-            @pl.when(jnp.logical_and(u > me, has_right))
-            def _():
-                j = n + me - u
-                mine = term(q, j)
-
-                @pl.when(has_left)
-                def _():
-                    sum_right(q, j).wait_recv()
-                    right_sum[q, j] = (mine + right_sum[q, j].astype(F32)).astype(BF16)
-
-                @pl.when(jnp.logical_not(has_left))
-                def _():
-                    right_sum[q, j] = mine.astype(BF16)
-
-                sum_right(q, j).start()
-
-            @pl.when(jnp.logical_and(u > n - 1 - me, has_left))
-            def _():
-                j = u - n + me
-                mine = term(q, j)
-
-                @pl.when(has_right)
-                def _():
-                    sum_left(q, j).wait_recv()
-                    left_sum[q, j] = (mine + left_sum[q, j].astype(F32)).astype(BF16)
-
-                @pl.when(jnp.logical_not(has_right))
-                def _():
-                    left_sum[q, j] = mine.astype(BF16)
-
-                sum_left(q, j).start()
-
-            return carry
-
-        lax.fori_loop(1, n, slot, 0)
-
+    def slot(q, u):
+        from_left = u <= me
+        from_right = u <= n - 1 - me
+        left_block, right_block = jnp.maximum(me - u, 0), jnp.minimum(me + u, n - 1)
+
+        @pl.when(from_left)
+        def _():
+            fwd_right(q, left_block).wait_recv()
+
+            @pl.when(has_right)
+            def _():
+                fwd_right(q, left_block).start()
+
+        @pl.when(from_right)
+        def _():
+            fwd_left(q, right_block).wait_recv()
+
+            @pl.when(has_left)
+            def _():
+                fwd_left(q, right_block).start()
+
+        @pl.when(jnp.logical_and(u > me, has_right))
+        def _():
+            j = n + me - u
+            mine = term(q, j)
+
+            @pl.when(has_left)
+            def _():
+                sum_right(q, j).wait_recv()
+                right_sum[q, j] = (mine + right_sum[q, j].astype(F32)).astype(BF16)
+
+            @pl.when(jnp.logical_not(has_left))
+            def _():
+                right_sum[q, j] = mine.astype(BF16)
+
+            sum_right(q, j).start()
+
+        @pl.when(jnp.logical_and(u > n - 1 - me, has_left))
+        def _():
+            j = u - n + me
+            mine = term(q, j)
+
+            @pl.when(has_right)
+            def _():
+                sum_left(q, j).wait_recv()
+                left_sum[q, j] = (mine + left_sum[q, j].astype(F32)).astype(BF16)
+
+            @pl.when(jnp.logical_not(has_right))
+            def _():
+                left_sum[q, j] = mine.astype(BF16)
+
+            sum_left(q, j).start()
+
+    back_copy = remote(
+        back_mine, back_other, pair_send.at[1], pair_recv.at[1], {"tensor": 1 - core}
+    )
+
+    def complete(q):
         cots = cot_buf[q].reshape(n * rows, part)
-        back = nt_dot(up[:, cols(q)], cots)
-        if q == 0:
-            back_mine[...] = back
-        else:
-            back_mine[...] += back
-        if q == PARTS - 1:
-            back_copy = remote(
-                back_mine, back_other, pair_send.at[1], pair_recv.at[1], {"tensor": 1 - core}
-            )
+        back_mine[...] += nt_dot(up[:, cols(q)], cots)
+
+        @pl.when(q == PARTS - 1)
+        def _():
             back_copy.start()
+
         full = jnp.dot(low_tr[...].astype(BF16), cots, preferred_element_type=F32)
         full = full.reshape(n_local, rank, part)
         for d in range(n_dp):
@@ -258,9 +251,27 @@
                 grad_out_buf[q, d] = piece.astype(BF16)
                 dp_copy(q, d).start()
 
-        if q > 0:
-            finish_out(q - 1)
-            finish_grad(q - 1)
+    back_mine[...] = jnp.zeros_like(back_mine)
+
+    def step(s, carry):
+        def one(q, inner):
+            slot(q, s - q)
+            return inner
+
+        lax.fori_loop(jnp.maximum(0, s - n + 1), jnp.minimum(PARTS, s), one, 0)
+
+        @pl.when(s >= n - 1)
+        def _():
+            complete(s - n + 1)
+
+        @pl.when(s >= n)
+        def _():
+            finish_out(s - n)
+            finish_grad(s - n)
+
+        return carry
+
+    lax.fori_loop(1, PARTS + n - 1, step, 0)
 
     finish_out(PARTS - 1)
     back_copy.wait_recv()
@@ -272,7 +283,9 @@
             both = back_mine[span, there] + back_other[span, there]
             both = (both * tab_buf[b, n_local + x : n_local + x + 1, :]).astype(BF16)
             projected = projected + nt_dot(pick[x, :, there], both)
-        hgrad[x] = nt_dot(projected.astype(BF16), frozen[x]).astype(BF16)
+        hgrad[x] = jnp.dot(
+            projected.astype(BF16), frozen[x], preferred_element_type=F32
+        ).astype(BF16)
     finish_grad(PARTS - 1)
 
     low_copy.wait_send()
@@ -352,7 +365,7 @@
         ),
     )(
         hidden.reshape(n_local, n * cap, half_ff),
-        frozen_a,
+        frozen_a.transpose(0, 2, 1),
         trained_b.reshape(ranks, width),
         tables,
         cotangent,

time: 78.9 us -> 68.5 us (0.87)
  Pallas kernels: 69.6 us -> 61.1 us
  local copies, waits for them, and re-layouts: 7.58 us -> 5.73 us
    pallas_call x1, Pallas kernels: 69.6 us -> 61.1 us  [local(): pl.pallas_call(functools.partial(kernel, (n, n_dp, n_local, rank, cap, ro...]
    unnamed x12 -> x11, local copies, waits for them, and re-layouts: 7.58 us -> 5.73 us
where the time goes in v3:
time: 68.5 us; the launch traced here: 68.2 us
  Pallas kernels  61.1 us (89%)
  local copies, waits for them, and re-layouts  5.73 us (8%)
    pallas_call x1, Pallas kernels, local(): pl.pallas_call(functools.partial(kernel, (n, n_dp, n_local, rank, cap, ro...  61.1 us
    unnamed x11, local copies, waits for them, and re-layouts  5.73 us

profile of v3, /device:TPU:0, one launch (start us, length us, event | category | flops | bytes accessed | tf_op | source)
XLA Modules:
  0.0 68.2 jit_solution(5973375461505187566)
XLA Ops:
  0.6 0.0 copy-start.2
  0.6 0.7 copy-done.2
  1.3 0.0 copy-start.3
  1.3 0.1 convolution_select_fusion
  1.5 0.5 copy-done.3
  2.0 0.6 pad_maximum_fusion.tables
  2.7 61.1 %shard_map.85 = (bf16[128,2048]{1,0:T(8,128)(2,1)}, f32[128,2048]{1,0:T(8,128)}, bf16[4,320,384]{2,1,0:T(8,128)(2,1)}) custom-call(bf16[4,320,384]{2,1,0:T(8,128)(2,1)} %bitcast.20, bf16[4,64,384]{2,1,0:T(8,128)(2,1)} %bitcast.21, bf16[256,2048]{1,0:T(8,128)(2,1)} %bitcast.19, f32[4,8,128]{2,1,0:T(8,128)} %pad_maximum_fusion.tables, bf16[128,2048]{1,0:T(8,128)(2,1)} %cot.1), custom_call_target="tpu_custom_call" | custom-call | flops 1610612736 | bytes 8388608 | tf_op jit(solution)/shard_map/pallas_call | solution.py:333
  63.7 0.0 copy-start
  63.7 2.0 %copy.14 = bf16[128,2048]{1,0:T(8,128)(2,1)} copy(bf16[128,2048]{1,0:T(8,128)(2,1)} %get-tuple-element.18) | data formatting | bytes 1048576
  65.7 0.0 copy-done
  65.7 0.0 copy-start.1
  65.7 1.0 %copy.15 = f32[4,32,2048]{2,1,0:T(8,128)} copy(f32[4,32,2048]{2,1,0:T(8,128)S(1)} %bitcast.12) | data formatting | bytes 2097152
  66.7 0.6 copy-done.1
  67.3 0.9 %copy.16 = bf16[4,1,4,80,384]{4,3,2,1,0:T(8,128)(2,1)} copy(bf16[4,1,4,80,384]{4,3,2,1,0:T(8,128)(2,1)S(1)} %bitcast.13) | data formatting | bytes 1966080
  (2 shorter events, 0.0 us)
Async XLA Ops:
  0.6 0.7 %copy-start.2 = (s32[128,8]{0,1:T(8,128)S(1)}, s32[128,8]{0,1:T(8,128)}, u32[]{:S(2)}) copy-start(s32[128,8]{0,1:T(8,128)} %param.9) | copy-start | bytes 12292
  1.3 0.7 %copy-start.3 = (f32[128,8]{0,1:T(8,128)S(1)}, f32[128,8]{0,1:T(8,128)}, u32[]{:S(2)}) copy-start(f32[128,8]{0,1:T(8,128)} %param.10) | copy-start | bytes 12292
  63.7 2.0 %copy-start = (f32[128,2048]{1,0:T(8,128)S(1)}, f32[128,2048]{1,0:T(8,128)}, u32[]{:S(2)}) copy-start(f32[128,2048]{1,0:T(8,128)} %get-tuple-element.7) | copy-start | bytes 3145732
  65.7 1.6 %copy-start.1 = (bf16[4,320,384]{2,1,0:T(8,128)(2,1)S(1)}, bf16[4,320,384]{2,1,0:T(8,128)(2,1)}, u32[]{:S(2)}) copy-start(bf16[4,320,384]{2,1,0:T(8,128)(2,1)} %get-tuple-element.8) | copy-start | bytes 2949124

commit v4 on v3

--- a/solution.py
+++ b/solution.py
@@ -10,28 +10,36 @@
 F32, BF16 = jnp.float32, jnp.bfloat16
 MESH = pl.DeviceIdType.MESH
 PARTS = 4
+LAG = 2
 
 
 def nt_dot(a, b):
     return lax.dot_general(a, b, (((1,), (1,)), ((), ())), preferred_element_type=F32)
 
 
-def token_tables(routes, gate_weights, experts_all, n_local):
-    rows = routes.shape[0]
-    ids = jnp.arange(experts_all, dtype=jnp.int32)
-    match = routes.T[:, None, :] == ids[None, :, None]
-    gates = jnp.sum(jnp.where(match, gate_weights.T[:, None, :], 0.0), axis=0)
-    hits = jnp.any(match, axis=0)
-    upper = jnp.triu(jnp.ones((rows, rows), BF16), 1)
+def fill_tables(tables, routes, gate_weights, n, n_local):
+    rows = routes.shape[1]
+    hit_rows, gate_rows = [], []
+    for e in range(n * n_local):
+        match = routes == e
+        hit_rows.append(jnp.sum(jnp.where(match, 1.0, 0.0), axis=0, keepdims=True))
+        gate_rows.append(jnp.sum(jnp.where(match, gate_weights, 0.0), axis=0, keepdims=True))
+    hits = jnp.concatenate(hit_rows, axis=0)
+    earlier = lax.broadcasted_iota(jnp.int32, (rows, rows), 0)
+    upper = earlier < lax.broadcasted_iota(jnp.int32, (rows, rows), 1)
+    upper = jnp.where(upper, 1.0, 0.0).astype(BF16)
     before = jnp.dot(hits.astype(BF16), upper, preferred_element_type=F32)
-    places = jnp.where(hits, before, -1.0).reshape(-1, n_local, rows)
-    return jnp.concatenate([places, gates.reshape(-1, n_local, rows)], axis=1)
+    places = jnp.where(hits > 0, before, -1.0)
+    for j in range(n):
+        tables[j, 0:n_local] = places[j * n_local : (j + 1) * n_local]
+        for x in range(n_local):
+            tables[j, n_local + x : n_local + x + 1] = gate_rows[j * n_local + x]
 
 
 def kernel(
-    dims, hidden, frozen, up, tables, cot, out, grad, hgrad,
-    cot_buf, right_sum, left_sum, tab_buf, low_mine, low_other, pick, low_tr, low_tok,
-    back_mine, back_other, grad_out_buf, grad_in_buf,
+    dims, hidden, frozen, up, routes, gate_weights, cot, out, grad, hgrad,
+    cot_buf, right_sum, left_sum, tables, tab_buf, low_mine, low_other, pick, low_f32, low_tr, low_tok,
+    proj, back_mine, back_other, grad_out_buf, grad_in_buf,
     tab_send, tab_recv, pair_send, pair_recv,
     fwd_r_send, fwd_l_send, fwd_recv, sum_r_send, sum_l_send, sum_r_recv, sum_l_recv,
     dp_send, dp_recv,
@@ -96,6 +104,7 @@
     pl.semaphore_signal(barrier, inc=1, device_id={"tensor": 1 - core}, device_id_type=MESH)
     for q in range(PARTS):
         cot_buf[q, me] = cot[:, q * part : (q + 1) * part]
+    fill_tables(tables, routes[...], gate_weights[...], n, n_local)
     tab_buf[me] = tables[me]
     pl.semaphore_wait(barrier, n + n_dp - 1)
 
@@ -110,8 +119,39 @@
         def _():
             fwd_left(q, me).start()
 
+    def forward(q, u):
+        from_left = u <= me
+        from_right = u <= n - 1 - me
+        left_block, right_block = jnp.maximum(me - u, 0), jnp.minimum(me + u, n - 1)
+
+        @pl.when(from_left)
+        def _():
+            fwd_right(q, left_block).wait_recv()
+
+            @pl.when(has_right)
+            def _():
+                fwd_right(q, left_block).start()
+
+        @pl.when(from_right)
+        def _():
+            fwd_left(q, right_block).wait_recv()
+
+            @pl.when(has_left)
+            def _():
+                fwd_left(q, right_block).start()
+
+    def wave(work, s):
+        def one(q, inner):
+            work(q, s - q)
+            return inner
+
+        lax.fori_loop(jnp.maximum(0, s - n + 1), jnp.minimum(PARTS, s), one, 0)
+
+    def forward_step(s):
+        wave(forward, s)
+
     for x in range(n_local):
-        low_mine[x * rank : (x + 1) * rank, :] = nt_dot(frozen[x], hidden[x])
+        low_mine[:, x * rank : (x + 1) * rank] = nt_dot(hidden[x], frozen[x])
     low_copy = remote(
         low_mine, low_other, pair_send.at[0], pair_recv.at[0], {"tensor": 1 - core}
     )
@@ -122,23 +162,26 @@
         remote(
             tables.at[j], tab_buf.at[j], tab_send.at[k], tab_recv.at[j], {"expert": j}
         ).wait_recv()
-    slots = lax.broadcasted_iota(jnp.int32, (n * cap, rows), 0).astype(F32)
+    slot_row = lax.broadcasted_iota(jnp.int32, (cap, rows), 0).astype(F32)
+    slot_col = lax.broadcasted_iota(jnp.int32, (rows, cap), 1).astype(F32)
     for b in range(n):
         tab = tab_buf[b]
         for x in range(n_local):
-            want = jnp.where(tab[x : x + 1] >= 0, tab[x : x + 1] + b * cap, -1.0)
-            pick[x, :, b * rows : (b + 1) * rows] = jnp.where(slots == want, 1.0, 0.0).astype(BF16)
+            pick[x, b] = jnp.where(slot_row == tab[x : x + 1], 1.0, 0.0).astype(BF16)
     low_copy.wait_recv()
-    for x in range(n_local):
-        span = slice(x * rank, (x + 1) * rank)
-        low = (low_mine[span, :] + low_other[span, :]).astype(BF16)
-        for b in range(n):
-            there = slice(b * rows, (b + 1) * rows)
-            chosen = jnp.dot(low, pick[x, :, there], preferred_element_type=F32)
-            gated = chosen * tab_buf[b, n_local + x : n_local + x + 1, :]
-            low_tr[span, there] = gated
     for b in range(n):
-        low_tok[b] = low_tr[:, b * rows : (b + 1) * rows].T.astype(BF16)
+        if b % 2 == 0 and b // 2 < LAG:
+            forward_step(b // 2 + 1)
+        down = tab_buf[b].T
+        there = slice(b * cap, (b + 1) * cap)
+        low = (low_mine[there, :] + low_other[there, :]).astype(BF16)
+        for x in range(n_local):
+            span = slice(x * rank, (x + 1) * rank)
+            chosen = jnp.where(slot_col == down[:, x : x + 1], 1.0, 0.0).astype(BF16)
+            rows_low = jnp.dot(chosen, low[:, span], preferred_element_type=F32)
+            low_f32[:, span] = rows_low * down[:, n_local + x : n_local + x + 1]
+        low_tok[b] = low_f32[...].astype(BF16)
+        low_tr[:, b * rows : (b + 1) * rows] = low_f32[...].T.astype(BF16)
 
     def term(q, j):
         return jnp.dot(low_tok[j], up[:, cols(q)], preferred_element_type=F32)
@@ -172,27 +215,7 @@
             dp_arrival(q, d).wait_recv()
             grad[:, cols(q)] += grad_in_buf[q, d].astype(F32)
 
-    def slot(q, u):
-        from_left = u <= me
-        from_right = u <= n - 1 - me
-        left_block, right_block = jnp.maximum(me - u, 0), jnp.minimum(me + u, n - 1)
-
-        @pl.when(from_left)
-        def _():
-            fwd_right(q, left_block).wait_recv()
-
-            @pl.when(has_right)
-            def _():
-                fwd_right(q, left_block).start()
-
-        @pl.when(from_right)
-        def _():
-            fwd_left(q, right_block).wait_recv()
-
-            @pl.when(has_left)
-            def _():
-                fwd_left(q, right_block).start()
-
+    def add_sums(q, u):
         @pl.when(jnp.logical_and(u > me, has_right))
         def _():
             j = n + me - u
@@ -237,7 +260,7 @@
         def _():
             back_copy.start()
 
-        full = jnp.dot(low_tr[...].astype(BF16), cots, preferred_element_type=F32)
+        full = jnp.dot(low_tr[...], cots, preferred_element_type=F32)
         full = full.reshape(n_local, rank, part)
         for d in range(n_dp):
             piece = full[:, d * share : (d + 1) * share].reshape(n_local * share, part)
@@ -252,13 +275,11 @@
                 dp_copy(q, d).start()
 
     back_mine[...] = jnp.zeros_like(back_mine)
+    last = PARTS + n - 2
 
     def step(s, carry):
-        def one(q, inner):
-            slot(q, s - q)
-            return inner
-
-        lax.fori_loop(jnp.maximum(0, s - n + 1), jnp.minimum(PARTS, s), one, 0)
+        forward_step(s)
+        wave(add_sums, s - LAG)
 
         @pl.when(s >= n - 1)
         def _():
@@ -266,27 +287,36 @@
 
         @pl.when(s >= n)
         def _():
-            finish_out(s - n)
             finish_grad(s - n)
 
+        @pl.when(s >= n + LAG)
+        def _():
+            finish_out(s - n - LAG)
+
         return carry
 
-    lax.fori_loop(1, PARTS + n - 1, step, 0)
-
-    finish_out(PARTS - 1)
-    back_copy.wait_recv()
-    for x in range(n_local):
-        span = slice(x * rank, (x + 1) * rank)
-        projected = jnp.zeros((n * cap, rank), F32)
-        for b in range(n):
-            there = slice(b * rows, (b + 1) * rows)
-            both = back_mine[span, there] + back_other[span, there]
-            both = (both * tab_buf[b, n_local + x : n_local + x + 1, :]).astype(BF16)
-            projected = projected + nt_dot(pick[x, :, there], both)
-        hgrad[x] = jnp.dot(
-            projected.astype(BF16), frozen[x], preferred_element_type=F32
-        ).astype(BF16)
-    finish_grad(PARTS - 1)
+    lax.fori_loop(LAG + 1, last + 1, step, 0)
+    for s in range(last + 1, last + LAG + 1):
+        wave(add_sums, s - LAG)
+        if s == last + 1:
+            back_copy.wait_recv()
+            for b in range(n):
+                for x in range(n_local):
+                    span, there = slice(x * rank, (x + 1) * rank), slice(b * rows, (b + 1) * rows)
+                    both = back_mine[span, there] + back_other[span, there]
+                    both = (both * tab_buf[b, n_local + x : n_local + x + 1, :]).astype(BF16)
+                    proj[b * cap : (b + 1) * cap, span] = nt_dot(pick[x, b], both)
+        if s == last + LAG:
+            for x in range(n_local):
+                hgrad[x] = jnp.dot(
+                    proj[:, x * rank : (x + 1) * rank].astype(BF16), frozen[x],
+                    preferred_element_type=F32,
+                ).astype(BF16)
+            finish_grad(PARTS - 1)
+        if s - n - LAG >= 0:
+            finish_out(s - n - LAG)
+    for q in range(max(0, last - n + 1), PARTS):
+        finish_out(q)
 
     low_copy.wait_send()
     back_copy.wait_send()
@@ -326,7 +356,6 @@
     share = rank // n_dp
     part = width // PARTS
     ranks = n_local * rank
-    tables = token_tables(routes, gate_weights, n_local * n, n_local)
     vmem = pl.BlockSpec(memory_space=pltpu.VMEM)
     dma = pltpu.SemaphoreType.DMA
     grid_sem = dma((PARTS, n))
@@ -337,18 +366,21 @@
             jax.ShapeDtypeStruct((n_local * share, width), F32),
             jax.ShapeDtypeStruct((n_local, n * cap, half_ff), BF16),
         ),
-        in_specs=[vmem] * 5,
+        in_specs=[vmem] * 6,
         out_specs=(vmem,) * 3,
         scratch_shapes=[
             pltpu.VMEM((PARTS, n, rows, part), BF16),
             pltpu.VMEM((PARTS, n, rows, part), BF16),
             pltpu.VMEM((PARTS, n, rows, part), BF16),
             pltpu.VMEM((n, 2 * n_local, rows), F32),
-            pltpu.VMEM((ranks, n * cap), F32),
-            pltpu.VMEM((ranks, n * cap), F32),
-            pltpu.VMEM((n_local, n * cap, n * rows), BF16),
-            pltpu.VMEM((ranks, n * rows), F32),
+            pltpu.VMEM((n, 2 * n_local, rows), F32),
+            pltpu.VMEM((n * cap, ranks), F32),
+            pltpu.VMEM((n * cap, ranks), F32),
+            pltpu.VMEM((n_local, n, cap, rows), BF16),
+            pltpu.VMEM((rows, ranks), F32),
+            pltpu.VMEM((ranks, n * rows), BF16),
             pltpu.VMEM((n, rows, ranks), BF16),
+            pltpu.VMEM((n * cap, ranks), F32),
             pltpu.VMEM((ranks, n * rows), F32),
             pltpu.VMEM((ranks, n * rows), F32),
             pltpu.VMEM((PARTS, n_dp, n_local * share, part), BF16),
@@ -367,7 +399,8 @@
         hidden.reshape(n_local, n * cap, half_ff),
         frozen_a.transpose(0, 2, 1),
         trained_b.reshape(ranks, width),
-        tables,
+        routes.T,
+        gate_weights.T,
         cotangent,
     )
     return (

time: 68.5 us -> 78.6 us (1.15)
  Pallas kernels: 61.1 us -> 73.2 us
  local copies, waits for them, and re-layouts: 5.73 us -> 4.5 us
    pallas_call x1, Pallas kernels: 61.1 us -> 73.2 us  [local(): pl.pallas_call(functools.partial(kernel, (n, n_dp, n_local, rank, cap, ro...]
    unnamed x11 -> x7, local copies, waits for them, and re-layouts: 5.73 us -> 4.5 us
where the time goes in v4:
time: 78.6 us; the launch traced here: 78.3 us
  Pallas kernels  73.2 us (93%)
  local copies, waits for them, and re-layouts  4.5 us (6%)
    pallas_call x1, Pallas kernels, local(): pl.pallas_call(functools.partial(kernel, (n, n_dp, n_local, rank, cap, ro...  73.2 us
    unnamed x7, local copies, waits for them, and re-layouts  4.5 us

profile of v4, /device:TPU:0, one launch (start us, length us, event | category | flops | bytes accessed | tf_op | source)
XLA Modules:
  0.0 78.3 jit_solution(9299383776999245671)
XLA Ops:
  0.6 73.2 %shard_map.85 = (bf16[128,2048]{1,0:T(8,128)(2,1)}, f32[128,2048]{1,0:T(8,128)}, bf16[4,320,384]{2,1,0:T(8,128)(2,1)}) custom-call(bf16[4,320,384]{2,1,0:T(8,128)(2,1)} %bitcast.12, bf16[4,64,384]{2,1,0:T(8,128)(2,1)} %bitcast.13, bf16[256,2048]{1,0:T(8,128)(2,1)} %bitcast.11, s32[8,128]{1,0:T(8,128)} %bitcast.14, f32[8,128]{1,0:T(8,128)} %bitcast.15, ...), custom_call_target="tpu_custom_call" | custom-call | flops 1610612736 | bytes 8388608 | tf_op jit(solution)/shard_map/pallas_call | solution.py:362
  73.8 0.0 copy-start
  73.9 2.0 %copy.13 = bf16[128,2048]{1,0:T(8,128)(2,1)} copy(bf16[128,2048]{1,0:T(8,128)(2,1)} %get-tuple-element.15) | data formatting | bytes 1048576
  75.8 0.0 copy-done
  75.8 0.0 copy-start.1
  75.8 1.0 %copy.14 = f32[4,32,2048]{2,1,0:T(8,128)} copy(f32[4,32,2048]{2,1,0:T(8,128)S(1)} %bitcast.9) | data formatting | bytes 2097152
  76.8 0.6 copy-done.1
  77.4 0.9 %copy.15 = bf16[4,1,4,80,384]{4,3,2,1,0:T(8,128)(2,1)} copy(bf16[4,1,4,80,384]{4,3,2,1,0:T(8,128)(2,1)S(1)} %bitcast.10) | data formatting | bytes 1966080
Async XLA Ops:
  73.8 2.0 %copy-start = (f32[128,2048]{1,0:T(8,128)S(1)}, f32[128,2048]{1,0:T(8,128)}, u32[]{:S(2)}) copy-start(f32[128,2048]{1,0:T(8,128)} %get-tuple-element.7) | copy-start | bytes 3145732
  75.8 1.6 %copy-start.1 = (bf16[4,320,384]{2,1,0:T(8,128)(2,1)S(1)}, bf16[4,320,384]{2,1,0:T(8,128)(2,1)}, u32[]{:S(2)}) copy-start(bf16[4,320,384]{2,1,0:T(8,128)(2,1)} %get-tuple-element.8) | copy-start | bytes 2949124

commit v5 on v4

--- a/solution.py
+++ b/solution.py
@@ -9,8 +9,7 @@
 
 F32, BF16 = jnp.float32, jnp.bfloat16
 MESH = pl.DeviceIdType.MESH
-PARTS = 4
-LAG = 2
+PARTS = 2
 
 
 def nt_dot(a, b):
@@ -147,8 +146,9 @@
 
         lax.fori_loop(jnp.maximum(0, s - n + 1), jnp.minimum(PARTS, s), one, 0)
 
-    def forward_step(s):
-        wave(forward, s)
+    def exchange(q, u):
+        add_sums(q, u)
+        forward(q, u)
 
     for x in range(n_local):
         low_mine[:, x * rank : (x + 1) * rank] = nt_dot(hidden[x], frozen[x])
@@ -170,8 +170,6 @@
             pick[x, b] = jnp.where(slot_row == tab[x : x + 1], 1.0, 0.0).astype(BF16)
     low_copy.wait_recv()
     for b in range(n):
-        if b % 2 == 0 and b // 2 < LAG:
-            forward_step(b // 2 + 1)
         down = tab_buf[b].T
         there = slice(b * cap, (b + 1) * cap)
         low = (low_mine[there, :] + low_other[there, :]).astype(BF16)
@@ -278,8 +276,7 @@
     last = PARTS + n - 2
 
     def step(s, carry):
-        forward_step(s)
-        wave(add_sums, s - LAG)
+        wave(exchange, s)
 
         @pl.when(s >= n - 1)
         def _():
@@ -288,35 +285,25 @@
         @pl.when(s >= n)
         def _():
             finish_grad(s - n)
-
-        @pl.when(s >= n + LAG)
-        def _():
-            finish_out(s - n - LAG)
+            finish_out(s - n)
 
         return carry
 
-    lax.fori_loop(LAG + 1, last + 1, step, 0)
-    for s in range(last + 1, last + LAG + 1):
-        wave(add_sums, s - LAG)
-        if s == last + 1:
-            back_copy.wait_recv()
-            for b in range(n):
-                for x in range(n_local):
-                    span, there = slice(x * rank, (x + 1) * rank), slice(b * rows, (b + 1) * rows)
-                    both = back_mine[span, there] + back_other[span, there]
-                    both = (both * tab_buf[b, n_local + x : n_local + x + 1, :]).astype(BF16)
-                    proj[b * cap : (b + 1) * cap, span] = nt_dot(pick[x, b], both)
-        if s == last + LAG:
-            for x in range(n_local):
-                hgrad[x] = jnp.dot(
-                    proj[:, x * rank : (x + 1) * rank].astype(BF16), frozen[x],
-                    preferred_element_type=F32,
-                ).astype(BF16)
-            finish_grad(PARTS - 1)
-        if s - n - LAG >= 0:
-            finish_out(s - n - LAG)
-    for q in range(max(0, last - n + 1), PARTS):
-        finish_out(q)
+    lax.fori_loop(1, last + 1, step, 0)
+    finish_out(PARTS - 1)
+    back_copy.wait_recv()
+    for b in range(n):
+        for x in range(n_local):
+            span, there = slice(x * rank, (x + 1) * rank), slice(b * rows, (b + 1) * rows)
+            both = back_mine[span, there] + back_other[span, there]
+            both = (both * tab_buf[b, n_local + x : n_local + x + 1, :]).astype(BF16)
+            proj[b * cap : (b + 1) * cap, span] = nt_dot(pick[x, b], both)
+    for x in range(n_local):
+        hgrad[x] = jnp.dot(
+            proj[:, x * rank : (x + 1) * rank].astype(BF16), frozen[x],
+            preferred_element_type=F32,
+        ).astype(BF16)
+    finish_grad(PARTS - 1)
 
     low_copy.wait_send()
     back_copy.wait_send()

time: 78.6 us -> 63.4 us (0.81)
  Pallas kernels: 73.2 us -> 58.1 us
    pallas_call x1, Pallas kernels: 73.2 us -> 58.1 us  [local(): pl.pallas_call(functools.partial(kernel, (n, n_dp, n_local, rank, cap, ro...]
where the time goes in v5:
time: 63.4 us; the launch traced here: 63.2 us
  Pallas kernels  58.1 us (92%)
  local copies, waits for them, and re-layouts  4.5 us (7%)
  between operations  0.65 us (1%)
    pallas_call x1, Pallas kernels, local(): pl.pallas_call(functools.partial(kernel, (n, n_dp, n_local, rank, cap, ro...  58.1 us
    unnamed x7, local copies, waits for them, and re-layouts  4.5 us

profile of v5, /device:TPU:0, one launch (start us, length us, event | category | flops | bytes accessed | tf_op | source)
XLA Modules:
  0.0 63.2 jit_solution(10341938188730830208)
XLA Ops:
  0.6 58.1 %shard_map.85 = (bf16[128,2048]{1,0:T(8,128)(2,1)}, f32[128,2048]{1,0:T(8,128)}, bf16[4,320,384]{2,1,0:T(8,128)(2,1)}) custom-call(bf16[4,320,384]{2,1,0:T(8,128)(2,1)} %bitcast.12, bf16[4,64,384]{2,1,0:T(8,128)(2,1)} %bitcast.13, bf16[256,2048]{1,0:T(8,128)(2,1)} %bitcast.11, s32[8,128]{1,0:T(8,128)} %bitcast.14, f32[8,128]{1,0:T(8,128)} %bitcast.15, ...), custom_call_target="tpu_custom_call" | custom-call | flops 1610612736 | bytes 8388608 | tf_op jit(solution)/shard_map/pallas_call | solution.py:349
  58.7 0.0 copy-start
  58.7 2.0 %copy.13 = bf16[128,2048]{1,0:T(8,128)(2,1)} copy(bf16[128,2048]{1,0:T(8,128)(2,1)} %get-tuple-element.15) | data formatting | bytes 1048576
  60.7 0.0 copy-done
  60.7 0.0 copy-start.1
  60.7 1.0 %copy.14 = f32[4,32,2048]{2,1,0:T(8,128)} copy(f32[4,32,2048]{2,1,0:T(8,128)S(1)} %bitcast.9) | data formatting | bytes 2097152
  61.7 0.6 copy-done.1
  62.3 0.9 %copy.15 = bf16[4,1,4,80,384]{4,3,2,1,0:T(8,128)(2,1)} copy(bf16[4,1,4,80,384]{4,3,2,1,0:T(8,128)(2,1)S(1)} %bitcast.10) | data formatting | bytes 1966080
Async XLA Ops:
  58.7 2.0 %copy-start = (f32[128,2048]{1,0:T(8,128)S(1)}, f32[128,2048]{1,0:T(8,128)}, u32[]{:S(2)}) copy-start(f32[128,2048]{1,0:T(8,128)} %get-tuple-element.7) | copy-start | bytes 3145732
  60.7 1.6 %copy-start.1 = (bf16[4,320,384]{2,1,0:T(8,128)(2,1)S(1)}, bf16[4,320,384]{2,1,0:T(8,128)(2,1)}, u32[]{:S(2)}) copy-start(bf16[4,320,384]{2,1,0:T(8,128)(2,1)} %get-tuple-element.8) | copy-start | bytes 2949124
